TPU v7x, 256 devices: a whole 4x4x8 slice. The times are simulated.
256 devices in a mesh: shot: 32 (over y, z_hi, x), rcv: 8 (over z_lo, core).
Axes of the slice: x: 4, y: 4, z: 8 (z_hi: 2, z_lo: 4; z = z_hi * 4 + z_lo), core: 2. Of those that a mesh axis runs over, the one named last changes fastest.
Arguments:
- data: bfloat16 [2, 8, 4096, 4096], P(None, None, 'shot', 'rcv'), may hold values from -3 to 3
- inverse_wavelet: float32 [2, 8], replicated, may hold values from -1.5 to 1.5
- panel_blocks: int32 [2], replicated, may hold values from 0 to 31, as said below
Outputs:
- multiples: bfloat16 [16, 4096, 4096], P(None, 'shot', 'rcv')
Inputs may be any that keep to these rules, and one draw needn't show every extreme that they name: `panel_blocks`: the panels' blocks are distinct, and one of them is always the last block, 31.
All inputs are finite; a program needn't handle non-finite values.
Results may differ from a plain program's by a relative error of at most 0.001.
Values may be sent and summed in bfloat16 or wider, within the bound.
A program may use at most 64 MiB of HBM per device.

v0:
```python
import functools
import math

import jax
import jax.numpy as jnp
from jax import lax
from jax.experimental import pallas as pl
from jax.experimental.pallas import tpu as pltpu
from jax.sharding import PartitionSpec as P

MESH = pl.DeviceIdType.MESH
LAST = 31
NF, SIDE, LANES = 8, 128, 128
PARTS = 1
PIECES = 4 * PARTS
PIECE = (SIDE, LANES) if PARTS == 2 else (2, SIDE, LANES)
PERIOD = 2
COLS = 4
STEPS = ((1, 0), (0, 1), (-1, 0), (0, -1))

TREE = (
    (0, 0, 0), (1, 0, 1), (1, 0, 3), (1, 0, 0), (2, 0, 0), (1, 1, 2), (1, 1, 0), (1, 3, 2),
    (1, 1, 1), (2, 0, 3), (2, 3, 0), (1, 2, 2), (1, 2, 0), (2, 1, 0), (2, 2, 0),
)
OTHER = (
    ((1, 3), 2, (
        (1, 3, 0), (1, 3, 1), (1, 3, 3), (1, 3, 2), (0, 3, 1), (0, 3, 2), (1, 2, 0), (1, 2, 2),
        (1, 2, 3), (2, 3, 1), (0, 2, 2), (0, 0, 2), (2, 2, 3), (0, 2, 3), (3, 2, 3),
    )),
    ((1, 0), 1, (
        (1, 0, 0), (1, 0, 3), (1, 0, 1), (1, 0, 2), (1, 3, 2), (1, 1, 2), (1, 3, 0), (1, 3, 3),
        (2, 0, 1), (0, 0, 2), (0, 1, 2), (0, 3, 3), (2, 3, 3), (2, 3, 0), (2, 2, 0),
    )),
)
SKEW = 2
CROSS = 2


def tables(root, edges, base):
    depth = {root: base}
    while len(depth) < 16:
        for x, y, d in edges:
            if (x, y) in depth:
                there = ((x + STEPS[d][0]) % 4, (y + STEPS[d][1]) % 4)
                depth.setdefault(there, depth[(x, y)] + 1)
    masks = [sum(1 << (x * 4 + y) for x, y, d in edges if d == way) for way in range(4)]
    bits = [
        sum(1 << (x * 4 + y) for (x, y), v in depth.items() if (v >> i) & 1) for i in range(4)
    ]
    return masks, bits


HOME = tables((0, 0), TREE, 0)
AWAY = [tables(root, edges, base + CROSS) for root, base, edges in OTHER]
GATES = [root[0] * 4 + root[1] for root, base, edges in OTHER]


def place_of(block):
    return block % 4, block // 8, (block // 4) % 2


def bit(mask, place):
    return (mask >> place) & 1


def gather_kernel(block, data, rows, cols, table, row_recv, row_send, col_recv, col_send):
    shot, rcv = lax.axis_index("shot"), lax.axis_index("rcv")
    x, half, y = shot % 4, (shot // 4) % 2, shot // 8
    run, core = rcv // 2, rcv % 2

    def at(px, py, ph):
        return (py * 2 + ph) * 4 + px

    beside = [(at((x + a + 4) % 4, (y + b + 4) % 4, half), rcv) for a, b in STEPS]
    ways = beside + [(at(x, y, 1 - half), rcv)]
    col_ways = [(shot, rcv + 2), (shot, rcv - 2), (shot, run * 2 + 1 - core)]

    barrier = pltpu.get_barrier_semaphore()
    for device in ways + [col_ways[2]]:
        pl.semaphore_signal(barrier, inc=1, device_id=device, device_id_type=MESH)

    @pl.when(run < 3)
    def _():
        pl.semaphore_signal(barrier, inc=1, device_id=col_ways[0], device_id_type=MESH)

    @pl.when(run > 0)
    def _():
        pl.semaphore_signal(barrier, inc=1, device_id=col_ways[1], device_id_type=MESH)

    def either(p, values):
        return jnp.where(p == 0, values[0], values[1])

    blocks = (block, LAST)
    places = [place_of(b) for b in blocks]

    def piece(p, f, k):
        return rows.at[p, f, k]

    def copy(p, f, k, way):
        return pltpu.make_async_remote_copy(
            src_ref=piece(p, f, k), dst_ref=piece(p, f, k),
            send_sem=row_send.at[p, f, way], recv_sem=row_recv.at[p, f, k],
            device_id=ways[way], device_id_type=MESH,
        )

    per_col = NF // COLS

    def col_piece(p, i):
        return cols.at[p, :, pl.ds(i * per_col, per_col)]

    def col_copy(p, i, way):
        return pltpu.make_async_remote_copy(
            src_ref=col_piece(p, i), dst_ref=col_piece(p, i),
            send_sem=col_send.at[p, way], recv_sem=col_recv.at[p, i],
            device_id=col_ways[way], device_id_type=MESH,
        )

    def col_part(p):
        owner = either(p, [b // 4 for b in blocks])
        far = jnp.abs(run - owner // 2)
        mine = core == owner % 2
        goes_up = mine & (run >= owner // 2) & (run < 3)
        goes_down = mine & (run <= owner // 2) & (run > 0)
        return far, (goes_up, goes_down, mine)

    def own(p, _):
        @pl.when(shot == either(p, blocks))
        def _():
            def one(n, _):
                k, f = n // NF, n % NF
                lanes = pl.ds(pl.multiple_of((k // PARTS) * LANES, LANES), LANES)
                src = data.at[k % 2, f, :, lanes] if PARTS == 2 else data.at[:, f, :, lanes]
                pltpu.make_async_copy(src, piece(p, f, k), row_recv.at[p, f, k]).start()
                return 0
            lax.fori_loop(0, PIECES * NF, one, 0)

        @pl.when(rcv == either(p, [b // 4 for b in blocks]))
        def _():
            offset = either(p, [(b % 4) * SIDE for b in blocks])
            lanes = pl.ds(pl.multiple_of(offset, SIDE), SIDE)

            def one(i, _):
                src = data.at[:, pl.ds(i * per_col, per_col), :, lanes]
                pltpu.make_async_copy(src, col_piece(p, i), col_recv.at[p, i]).start()
                return 0
            lax.fori_loop(0, COLS, one, 0)
        return 0

    lax.fori_loop(0, 2, own, 0)

    def plan(n, _):
        f, p = n // 2, n % 2
        sx, sy, sh = (either(p, [place[i] for place in places]) for i in range(3))
        home = half == sh
        turn, other = f % 4, f // 4
        rx, ry = (x - sx + 4) % 4, (y - sy + 4) % 4
        nx, ny = (4 - rx) % 4, (4 - ry) % 4

        def turned(a, b, c, d):
            return jnp.where(turn == 0, a, jnp.where(turn == 1, b, jnp.where(turn == 2, c, d)))

        place = turned(rx, ry, nx, ny) * 4 + turned(ry, nx, ny, rx)

        def pick(part, i):
            away = jnp.where(other == 0, AWAY[0][part][i], AWAY[1][part][i])
            return bit(jnp.where(home, HOME[part][i], away), place)

        word = 0
        for way in range(4):
            word = word + (pick(0, way) << ((way + turn) % 4))
        gate = jnp.where(other == 0, GATES[0], GATES[1])
        word = word + jnp.where(home & (place == gate), 16, 0)
        late = SKEW * sum(pick(1, i) << i for i in range(4)) + other * (PERIOD // 2)
        table[n] = late * 32 + word
        return 0

    lax.fori_loop(0, 2 * NF, plan, 0)
    inner = jnp.where((run > 0) & (run < 3), 1, 0)
    pl.semaphore_wait(barrier, 7 + inner)

    def step(s, _):
        def stream(n, _):
            f, p = n // 2, n % 2
            word = table[n]
            left = s - word // 32

            @pl.when((left >= 0) & (left < PERIOD * PIECES) & (left % PERIOD == 0))
            def _():
                k = left // PERIOD
                copy(p, f, k, 0).wait_recv()
                for way in range(5):
                    @pl.when((word // 2**way) % 2 == 1)
                    def _(way=way):
                        copy(p, f, k, way).start()
            return 0

        lax.fori_loop(0, 2 * NF, stream, 0)

        def column(p, _):
            far, goes = col_part(p)
            i = s - 1 - 2 * far

            @pl.when(goes[2] & (i >= 0) & (i < COLS))
            def _():
                col_copy(p, i, 2).wait_recv()
                for way in range(3):
                    @pl.when(goes[way])
                    def _(way=way):
                        col_copy(p, i, way).start()
            return 0

        lax.fori_loop(0, 2, column, 0)
        return 0

    lax.fori_loop(0, PERIOD * PIECES + 8 * SKEW, step, 0)

    def rest(p, _):
        goes = col_part(p)[1]

        @pl.when(jnp.logical_not(goes[2]))
        def _():
            def one(i, _):
                col_copy(p, i, 2).wait_recv()
                return 0
            lax.fori_loop(0, COLS, one, 0)

        for way in range(3):
            @pl.when(goes[way])
            def _(way=way):
                pltpu.make_async_remote_copy(
                    src_ref=cols.at[p], dst_ref=cols.at[p],
                    send_sem=col_send.at[p, way], recv_sem=col_recv.at[p, 0],
                    device_id=col_ways[2], device_id_type=MESH,
                ).wait_send()
        return 0

    lax.fori_loop(0, 2, rest, 0)

    def sent(n, _):
        f, p = n // 2, n % 2
        word = table[n]
        for way in range(5):
            @pl.when((word // 2**way) % 2 == 1)
            def _(way=way):
                pltpu.make_async_remote_copy(
                    src_ref=rows.at[p, f], dst_ref=rows.at[p, f],
                    send_sem=row_send.at[p, f, way], recv_sem=row_recv.at[p, f, 0],
                    device_id=ways[way], device_id_type=MESH,
                ).wait_send()
        return 0

    lax.fori_loop(0, 2 * NF, sent, 0)


def gather(block, data):
    vmem = pl.BlockSpec(memory_space=pltpu.VMEM)
    return pl.pallas_call(
        functools.partial(gather_kernel, block),
        out_shape=(
            jax.ShapeDtypeStruct((2, NF, PIECES) + PIECE, data.dtype),
            jax.ShapeDtypeStruct((2,) + data.shape[:3] + (SIDE,), data.dtype),
        ),
        in_specs=[pl.BlockSpec(memory_space=pltpu.HBM)],
        out_specs=(vmem, vmem),
        scratch_shapes=[
            pltpu.SMEM((2 * NF,), jnp.int32),
            pltpu.SemaphoreType.DMA((2, NF, PIECES)),
            pltpu.SemaphoreType.DMA((2, NF, 5)),
            pltpu.SemaphoreType.DMA((2, COLS)),
            pltpu.SemaphoreType.DMA((2, 3)),
        ],
        compiler_params=pltpu.CompilerParams(
            collective_id=block, has_side_effects=True, vmem_limit_bytes=16 * 2**20
        ),
        name="gather",
    )(data)


def transform(re, im):
    def c(n):
        return math.cos(math.pi * n / 8)

    def s(n):
        return math.sin(math.pi * n / 8)

    a = c(2)
    quarter = []
    for t in range(4):
        main = (re[4], -im[4], -re[4], im[4])[t]
        last = re[8] if t % 2 == 0 else -re[8]
        quarter.append(main + last - im[8] * s(8 * t))
    d, e = a * (re[2] - re[6]), a * (im[2] + im[6])
    anti = [re[2] + re[6], d - e, im[6] - im[2], -d - e]
    even = [quarter[t] + anti[t] for t in range(4)] + [quarter[t] - anti[t] for t in range(4)]
    p1, q1, p3, q3 = re[1] + re[7], im[1] - im[7], re[3] + re[5], im[3] - im[5]
    m1, n1, m3, n3 = re[1] - re[7], im[1] + im[7], re[3] - re[5], im[3] + im[5]
    g, h = a * (p1 - p3), a * (q1 + q3)
    u, v = c(1) * m1 + s(1) * m3, s(1) * n1 + c(1) * n3
    w, z = s(1) * m1 - c(1) * m3, c(1) * n1 - s(1) * n3
    odd = [p1 + p3, u - v, g - h, w - z, q3 - q1, -w - z, -g - h, -u - v]
    return [even[t] + odd[t] for t in range(8)] + [even[t] - odd[t] for t in range(8)]


def multiply_kernel(wave, rows, cols, out, left, product):
    @pl.when(pl.program_id(0) == 0)
    def _():
        for f in range(NF):
            for p in range(2):
                lr, li = cols[p, 0, f], cols[p, 1, f]
                left[f, :SIDE, 2 * p * SIDE:(2 * p + 1) * SIDE] = lr
                left[f, :SIDE, (2 * p + 1) * SIDE:(2 * p + 2) * SIDE] = -li
                left[f, SIDE:, 2 * p * SIDE:(2 * p + 1) * SIDE] = li
                left[f, SIDE:, (2 * p + 1) * SIDE:(2 * p + 2) * SIDE] = lr

    for f in range(NF):
        right = jnp.concatenate([rows[p, f, c] if PARTS == 2 else rows[p, f, 0, c] for p in range(2) for c in range(2)], axis=0)
        product[f] = jnp.dot(left[f], right, preferred_element_type=jnp.float32)

    high = 16
    def tile(i, _):
        at = pl.ds(pl.multiple_of(i * high, high), high)
        at2 = pl.ds(pl.multiple_of(i * high + SIDE, high), high)
        re, im = [None], [None]
        for f in range(NF):
            pr, pi = product[f, at, :], product[f, at2, :]
            wr, wi = wave[0, f], wave[1, f]
            re.append(wr * pr - wi * pi)
            im.append(wr * pi + wi * pr)
        for t, sample in enumerate(transform(re, im)):
            out[t, at, :] = sample.astype(out.dtype)
        return 0

    lax.fori_loop(0, SIDE // high, tile, 0)


def multiply(wave, rows, cols):
    tile = LANES
    width = PIECES // PARTS * tile
    return pl.pallas_call(
        multiply_kernel,
        grid=(width // tile,),
        out_shape=jax.ShapeDtypeStruct((2 * NF, SIDE, width), rows.dtype),
        in_specs=[
            pl.BlockSpec(memory_space=pltpu.SMEM),
            pl.BlockSpec((2, NF, PARTS) + PIECE, lambda i: (0, 0, i) + (0,) * len(PIECE)),
            pl.BlockSpec((2, 2, NF, SIDE, SIDE), lambda i: (0, 0, 0, 0, 0)),
        ],
        out_specs=pl.BlockSpec((2 * NF, SIDE, tile), lambda i: (0, 0, i)),
        scratch_shapes=[
            pltpu.VMEM((NF, 2 * SIDE, 4 * SIDE), rows.dtype),
            pltpu.VMEM((NF, 2 * SIDE, tile), jnp.float32),
        ],
        compiler_params=pltpu.CompilerParams(vmem_limit_bytes=32 * 2**20),
        name="multiply",
    )(wave, rows, cols)


def shards(data, inverse_wavelet, panel_blocks):
    block = jnp.where(panel_blocks[0] == LAST, panel_blocks[1], panel_blocks[0])
    rows, cols = lax.switch(block, [functools.partial(gather, b) for b in range(LAST)], data)
    return multiply(inverse_wavelet * NF ** -0.5, rows, cols)


def solution(mesh):
    placed = (P(None, None, "shot", "rcv"), P(), P())
    return jax.shard_map(
        shards, mesh=mesh, in_specs=placed, out_specs=P(None, "shot", "rcv"), check_vma=False
    )
```

profile of v0, /device:TPU:33, one launch (start us, length us, event | category | flops | bytes accessed | tf_op | source)
XLA Modules:
  0.0 77.6 jit_solution(3554862186292092364)
XLA Ops:
  0.0 1.3 %fusion = (s32[1]{0:T(128)}, s32[1]{0:T(128)}) fusion(s32[2]{0:T(128)} %param.36), kind=kLoop, calls=%fused_computation.1 | loop fusion | bytes 16 | tf_op jit(solution)/shard_map/slice | solution.py:359
  3.2 0.0 copy-start
  3.2 67.3 %conditional.1 = ((bf16[2,8,4,2,128,128]{5,4,3,2,1,0:T(8,128)(2,1)}, bf16[2,2,8,128,128]{4,3,2,1,0:T(8,128)(2,1)S(1)})) conditional(s32[]{:T(128)} %clamp.3, bf16[2,8,128,512]{3,2,1,0:T(8,128)(2,1)} %param.34, bf16[2,8,128,512]{3,2,1,0:T(8,128)(2,1)} %param.34, bf16[2,8,128,512]{3,2,1,0:T(8,128)(2,1)} %param.34, ...), branch_computations={%region_0.1_spmd, %region_1.2_spmd, %region_2.3_spmd, %region_3.4_... | conditional | bytes 8 | solution.py:360
  3.4 67.0 %gather.61 = (bf16[2,8,4,2,128,128]{5,4,3,2,1,0:T(8,128)(2,1)}, bf16[2,2,8,128,128]{4,3,2,1,0:T(8,128)(2,1)S(1)}) custom-call(bf16[2,8,128,512]{3,2,1,0:T(8,128)(2,1)} %data.30), custom_call_target="tpu_custom_call" | custom-call | tf_op jit(solution)/shard_map/cond/branch_30_fun/gather/pallas_call | solution.py:257
  70.5 0.0 copy-done
  70.5 7.1 %multiply.1 = bf16[16,128,512]{2,1,0:T(8,128)(2,1)} custom-call(f32[2,8]{1,0:T(2,128)S(1)} %broadcast_multiply_fusion.wave, bf16[2,8,4,2,128,128]{5,4,3,2,1,0:T(8,128)(2,1)} %get-tuple-element.38.rows, bf16[2,2,8,128,128]{4,3,2,1,0:T(8,128)(2,1)S(1)} %get-tuple-element.39.cols), custom_call_target="tpu_custom_call" | custom-call | tf_op jit(solution)/shard_map/multiply/pallas_call | solution.py:339
  (1 shorter events, 0.0 us)
Async XLA Ops:
  3.2 67.3 %copy-start = (f32[2,8]{1,0:T(2,128)S(1)}, f32[2,8]{1,0:T(2,128)}, u32[]{:S(2)}) copy-start(f32[2,8]{1,0:T(2,128)} %param.35) | copy-start | bytes 196
where the time goes:
time: 77.8 us; the launch traced here: 77.6 us
  Pallas kernels  74.1 us (95%)
  between operations  1.9 us (2%)
  local copies, waits for them, and re-layouts  1.32 us (2%)
    pallas_call x1, Pallas kernels, gather(): pl.pallas_call(functools.partial(gather_kernel, block), out_shape=(jax.Sh...  67 us
    pallas_call x1, Pallas kernels, multiply(): pl.pallas_call(multiply_kernel, grid=(width // tile,), out_shape=jax.Shap...  7.06 us

commit v1 on v0

--- a/solution.py
+++ b/solution.py
@@ -11,10 +11,11 @@
 MESH = pl.DeviceIdType.MESH
 LAST = 31
 NF, SIDE, LANES = 8, 128, 128
-PARTS = 1
-PIECES = 4 * PARTS
-PIECE = (SIDE, LANES) if PARTS == 2 else (2, SIDE, LANES)
-PERIOD = 2
+PIECES = 4
+PIECE = (2, SIDE, LANES)
+TILES = 2
+SHIFT = 1
+PERIOD = 1 << SHIFT
 COLS = 4
 STEPS = ((1, 0), (0, 1), (-1, 0), (0, -1))
 
@@ -63,15 +64,15 @@
     return (mask >> place) & 1
 
 
-def gather_kernel(block, data, rows, cols, table, row_recv, row_send, col_recv, col_send):
+def gather_kernel(block, data, rows_hbm, cols, rows, lates, words, out_sem, row_recv, row_send, col_recv, col_send):
     shot, rcv = lax.axis_index("shot"), lax.axis_index("rcv")
-    x, half, y = shot % 4, (shot // 4) % 2, shot // 8
-    run, core = rcv // 2, rcv % 2
+    x, half, y = shot & 3, (shot >> 2) & 1, shot >> 3
+    run, core = rcv >> 1, rcv & 1
 
     def at(px, py, ph):
         return (py * 2 + ph) * 4 + px
 
-    beside = [(at((x + a + 4) % 4, (y + b + 4) % 4, half), rcv) for a, b in STEPS]
+    beside = [(at((x + a) & 3, (y + b) & 3, half), rcv) for a, b in STEPS]
     ways = beside + [(at(x, y, 1 - half), rcv)]
     col_ways = [(shot, rcv + 2), (shot, rcv - 2), (shot, run * 2 + 1 - core)]
 
@@ -117,19 +118,20 @@
 
     def col_part(p):
         owner = either(p, [b // 4 for b in blocks])
-        far = jnp.abs(run - owner // 2)
-        mine = core == owner % 2
-        goes_up = mine & (run >= owner // 2) & (run < 3)
-        goes_down = mine & (run <= owner // 2) & (run > 0)
+        o_run = owner >> 1
+        far = jnp.abs(run - o_run)
+        mine = core == (owner & 1)
+        goes_up = mine & (run >= o_run) & (run < 3)
+        goes_down = mine & (run <= o_run) & (run > 0)
         return far, (goes_up, goes_down, mine)
 
     def own(p, _):
         @pl.when(shot == either(p, blocks))
         def _():
             def one(n, _):
-                k, f = n // NF, n % NF
-                lanes = pl.ds(pl.multiple_of((k // PARTS) * LANES, LANES), LANES)
-                src = data.at[k % 2, f, :, lanes] if PARTS == 2 else data.at[:, f, :, lanes]
+                k, f = n >> 3, n & 7
+                lanes = pl.ds(pl.multiple_of(k * LANES, LANES), LANES)
+                src = data.at[:, f, :, lanes]
                 pltpu.make_async_copy(src, piece(p, f, k), row_recv.at[p, f, k]).start()
                 return 0
             lax.fori_loop(0, PIECES * NF, one, 0)
@@ -149,12 +151,12 @@
     lax.fori_loop(0, 2, own, 0)
 
     def plan(n, _):
-        f, p = n // 2, n % 2
+        f, p = n >> 1, n & 1
         sx, sy, sh = (either(p, [place[i] for place in places]) for i in range(3))
         home = half == sh
-        turn, other = f % 4, f // 4
-        rx, ry = (x - sx + 4) % 4, (y - sy + 4) % 4
-        nx, ny = (4 - rx) % 4, (4 - ry) % 4
+        turn, other = f & 3, f >> 2
+        rx, ry = (x - sx) & 3, (y - sy) & 3
+        nx, ny = -rx & 3, -ry & 3
 
         def turned(a, b, c, d):
             return jnp.where(turn == 0, a, jnp.where(turn == 1, b, jnp.where(turn == 2, c, d)))
@@ -167,11 +169,12 @@
 
         word = 0
         for way in range(4):
-            word = word + (pick(0, way) << ((way + turn) % 4))
+            word = word + (pick(0, way) << ((way + turn) & 3))
         gate = jnp.where(other == 0, GATES[0], GATES[1])
         word = word + jnp.where(home & (place == gate), 16, 0)
         late = SKEW * sum(pick(1, i) << i for i in range(4)) + other * (PERIOD // 2)
-        table[n] = late * 32 + word
+        lates[n] = late
+        words[n] = word
         return 0
 
     lax.fori_loop(0, 2 * NF, plan, 0)
@@ -180,16 +183,17 @@
 
     def step(s, _):
         def stream(n, _):
-            f, p = n // 2, n % 2
-            word = table[n]
-            left = s - word // 32
-
-            @pl.when((left >= 0) & (left < PERIOD * PIECES) & (left % PERIOD == 0))
+            left = s - lates[n]
+
+            @pl.when((left & ~(PERIOD * (PIECES - 1))) == 0)
             def _():
-                k = left // PERIOD
+                f, p = n >> 1, n & 1
+                k = left >> SHIFT
+                word = words[n]
                 copy(p, f, k, 0).wait_recv()
+                pltpu.make_async_copy(piece(p, f, k), rows_hbm.at[p, f, k], out_sem).start()
                 for way in range(5):
-                    @pl.when((word // 2**way) % 2 == 1)
+                    @pl.when((word & (1 << way)) != 0)
                     def _(way=way):
                         copy(p, f, k, way).start()
             return 0
@@ -198,7 +202,7 @@
 
         def column(p, _):
             far, goes = col_part(p)
-            i = s - 1 - 2 * far
+            i = s - 1 - 4 * far
 
             @pl.when(goes[2] & (i >= 0) & (i < COLS))
             def _():
@@ -214,6 +218,7 @@
 
     lax.fori_loop(0, PERIOD * PIECES + 8 * SKEW, step, 0)
 
+    pltpu.make_async_copy(rows, rows_hbm, out_sem).wait()
     def rest(p, _):
         goes = col_part(p)[1]
 
@@ -237,10 +242,10 @@
     lax.fori_loop(0, 2, rest, 0)
 
     def sent(n, _):
-        f, p = n // 2, n % 2
-        word = table[n]
+        f, p = n >> 1, n & 1
+        word = words[n]
         for way in range(5):
-            @pl.when((word // 2**way) % 2 == 1)
+            @pl.when((word & (1 << way)) != 0)
             def _(way=way):
                 pltpu.make_async_remote_copy(
                     src_ref=rows.at[p, f], dst_ref=rows.at[p, f],
@@ -253,17 +258,21 @@
 
 
 def gather(block, data):
-    vmem = pl.BlockSpec(memory_space=pltpu.VMEM)
+    vmem, hbm = (pl.BlockSpec(memory_space=m) for m in (pltpu.VMEM, pltpu.HBM))
+    landing = (2, NF, PIECES) + PIECE
     return pl.pallas_call(
         functools.partial(gather_kernel, block),
         out_shape=(
-            jax.ShapeDtypeStruct((2, NF, PIECES) + PIECE, data.dtype),
+            jax.ShapeDtypeStruct(landing, data.dtype),
             jax.ShapeDtypeStruct((2,) + data.shape[:3] + (SIDE,), data.dtype),
         ),
-        in_specs=[pl.BlockSpec(memory_space=pltpu.HBM)],
-        out_specs=(vmem, vmem),
+        in_specs=[hbm],
+        out_specs=(hbm, vmem),
         scratch_shapes=[
+            pltpu.VMEM(landing, data.dtype),
             pltpu.SMEM((2 * NF,), jnp.int32),
+            pltpu.SMEM((2 * NF,), jnp.int32),
+            pltpu.SemaphoreType.DMA,
             pltpu.SemaphoreType.DMA((2, NF, PIECES)),
             pltpu.SemaphoreType.DMA((2, NF, 5)),
             pltpu.SemaphoreType.DMA((2, COLS)),
@@ -301,64 +310,89 @@
     return [even[t] + odd[t] for t in range(8)] + [even[t] - odd[t] for t in range(8)]
 
 
-def multiply_kernel(wave, rows, cols, out, left, product):
-    @pl.when(pl.program_id(0) == 0)
-    def _():
+def multiply_kernel(wave, rows_hbm, cols, out, rows, left, product, staged, load_sem, sem):
+    loads = []
+    for i in range(PIECES // TILES):
+        some = pl.ds(i * TILES, TILES)
+        loads.append(
+            pltpu.make_async_copy(rows_hbm.at[:, :, some], rows.at[:, :, some], load_sem.at[i])
+        )
+        loads[i].start()
+
+    for f in range(NF):
+        for p in range(2):
+            lr, li = cols[p, 0, f], cols[p, 1, f]
+            left[f, :SIDE, 2 * p * SIDE:(2 * p + 1) * SIDE] = lr
+            left[f, :SIDE, (2 * p + 1) * SIDE:(2 * p + 2) * SIDE] = -li
+            left[f, SIDE:, 2 * p * SIDE:(2 * p + 1) * SIDE] = li
+            left[f, SIDE:, (2 * p + 1) * SIDE:(2 * p + 2) * SIDE] = lr
+
+    width = TILES * LANES
+    copies = []
+    for i in range(PIECES // TILES):
+        loads[i].wait()
         for f in range(NF):
-            for p in range(2):
-                lr, li = cols[p, 0, f], cols[p, 1, f]
-                left[f, :SIDE, 2 * p * SIDE:(2 * p + 1) * SIDE] = lr
-                left[f, :SIDE, (2 * p + 1) * SIDE:(2 * p + 2) * SIDE] = -li
-                left[f, SIDE:, 2 * p * SIDE:(2 * p + 1) * SIDE] = li
-                left[f, SIDE:, (2 * p + 1) * SIDE:(2 * p + 2) * SIDE] = lr
-
-    for f in range(NF):
-        right = jnp.concatenate([rows[p, f, c] if PARTS == 2 else rows[p, f, 0, c] for p in range(2) for c in range(2)], axis=0)
-        product[f] = jnp.dot(left[f], right, preferred_element_type=jnp.float32)
-
-    high = 16
-    def tile(i, _):
-        at = pl.ds(pl.multiple_of(i * high, high), high)
-        at2 = pl.ds(pl.multiple_of(i * high + SIDE, high), high)
-        re, im = [None], [None]
-        for f in range(NF):
-            pr, pi = product[f, at, :], product[f, at2, :]
-            wr, wi = wave[0, f], wave[1, f]
-            re.append(wr * pr - wi * pi)
-            im.append(wr * pi + wi * pr)
-        for t, sample in enumerate(transform(re, im)):
-            out[t, at, :] = sample.astype(out.dtype)
-        return 0
-
-    lax.fori_loop(0, SIDE // high, tile, 0)
+            right = jnp.concatenate(
+                [
+                    jnp.concatenate([rows[p, f, i * TILES + j, c] for j in range(TILES)], axis=1)
+                    for p in range(2)
+                    for c in range(2)
+                ],
+                axis=0,
+            )
+            product[f] = jnp.dot(left[f], right, preferred_element_type=jnp.float32)
+
+        high = 16
+
+        def tile(h, _, i=i):
+            at = pl.ds(pl.multiple_of(h * high, high), high)
+            at2 = pl.ds(pl.multiple_of(h * high + SIDE, high), high)
+            re, im = [None], [None]
+            for f in range(NF):
+                pr, pi = product[f, at, :], product[f, at2, :]
+                wr, wi = wave[0, f] * NF ** -0.5, wave[1, f] * NF ** -0.5
+                re.append(wr * pr - wi * pi)
+                im.append(wr * pi + wi * pr)
+            for t, sample in enumerate(transform(re, im)):
+                staged[i, t, at, :] = sample.astype(staged.dtype)
+            return 0
+
+        lax.fori_loop(0, SIDE // high, tile, 0)
+        copies.append(
+            pltpu.make_async_copy(
+                staged.at[i], out.at[:, :, pl.ds(i * width, width)], sem.at[i]
+            )
+        )
+        copies[i].start()
+    for copy in copies:
+        copy.wait()
 
 
 def multiply(wave, rows, cols):
-    tile = LANES
-    width = PIECES // PARTS * tile
+    width = TILES * LANES
+    vmem, hbm = (pl.BlockSpec(memory_space=m) for m in (pltpu.VMEM, pltpu.HBM))
     return pl.pallas_call(
         multiply_kernel,
-        grid=(width // tile,),
-        out_shape=jax.ShapeDtypeStruct((2 * NF, SIDE, width), rows.dtype),
-        in_specs=[
-            pl.BlockSpec(memory_space=pltpu.SMEM),
-            pl.BlockSpec((2, NF, PARTS) + PIECE, lambda i: (0, 0, i) + (0,) * len(PIECE)),
-            pl.BlockSpec((2, 2, NF, SIDE, SIDE), lambda i: (0, 0, 0, 0, 0)),
+        out_shape=jax.ShapeDtypeStruct((2 * NF, SIDE, PIECES * LANES), rows.dtype),
+        in_specs=[pl.BlockSpec(memory_space=pltpu.SMEM), hbm, vmem],
+        out_specs=hbm,
+        scratch_shapes=[
+            pltpu.VMEM(rows.shape, rows.dtype),
+            pltpu.VMEM((NF, 2 * SIDE, 4 * SIDE), rows.dtype),
+            pltpu.VMEM((NF, 2 * SIDE, width), jnp.float32),
+            pltpu.VMEM((PIECES // TILES, 2 * NF, SIDE, width), rows.dtype),
+            pltpu.SemaphoreType.DMA((PIECES // TILES,)),
+            pltpu.SemaphoreType.DMA((PIECES // TILES,)),
         ],
-        out_specs=pl.BlockSpec((2 * NF, SIDE, tile), lambda i: (0, 0, i)),
-        scratch_shapes=[
-            pltpu.VMEM((NF, 2 * SIDE, 4 * SIDE), rows.dtype),
-            pltpu.VMEM((NF, 2 * SIDE, tile), jnp.float32),
-        ],
-        compiler_params=pltpu.CompilerParams(vmem_limit_bytes=32 * 2**20),
+        compiler_params=pltpu.CompilerParams(vmem_limit_bytes=24 * 2**20),
         name="multiply",
     )(wave, rows, cols)
 
 
 def shards(data, inverse_wavelet, panel_blocks):
-    block = jnp.where(panel_blocks[0] == LAST, panel_blocks[1], panel_blocks[0])
+    block = jnp.min(panel_blocks)
     rows, cols = lax.switch(block, [functools.partial(gather, b) for b in range(LAST)], data)
-    return multiply(inverse_wavelet * NF ** -0.5, rows, cols)
+    return multiply(inverse_wavelet, rows, cols)
 
 
 def solution(mesh):

time: 77.8 us -> 72.4 us (0.931)
  the two profiles are of different devices: /device:TPU:33 before, /device:TPU:65 now
where the time goes in v1:
time: 72.4 us; the launch traced here: 72.3 us
  Pallas kernels  69.4 us (96%)
  other arithmetic  1.29 us (2%)
  between operations  0.86 us (1%)
  loops' own time  0.78 us (1%)
    pallas_call x1, Pallas kernels, gather(): pl.pallas_call(functools.partial(gather_kernel, block), out_shape=(jax.Sh...  63.4 us
    pallas_call x1, Pallas kernels, multiply(): pl.pallas_call(multiply_kernel, out_shape=jax.ShapeDtypeStruct((2 * NF, S...  5.99 us

profile of v1, /device:TPU:65, one launch (start us, length us, event | category | flops | bytes accessed | tf_op | source)
XLA Modules:
  0.0 72.3 jit_solution(5045770535823002271)
XLA Ops:
  0.0 1.3 %reduce_min.9 = s32[]{:T(128)} reduce(s32[2]{0:T(128)} %param.36, s32[]{:T(128)} %constant.1.clone.1), dimensions={0}, to_apply=%region_0.0 | reduce | flops 1 | bytes 16 | tf_op jit(solution)/shard_map/reduce_min | solution.py:393
  1.9 0.0 copy-start
  2.0 64.2 %conditional.1 = ((bf16[2,8,4,2,128,128]{5,4,3,2,1,0:T(8,128)(2,1)}, bf16[2,2,8,128,128]{4,3,2,1,0:T(8,128)(2,1)S(1)})) conditional(s32[]{:T(128)} %clamp.3, bf16[2,8,128,512]{3,2,1,0:T(8,128)(2,1)} %param.34, bf16[2,8,128,512]{3,2,1,0:T(8,128)(2,1)} %param.34, bf16[2,8,128,512]{3,2,1,0:T(8,128)(2,1)} %param.34, ...), branch_computations={%region_1.0_spmd, %region_2.0_spmd, %region_3.0_spmd, %region_4.0_... | conditional | bytes 8 | solution.py:394
  2.3 63.4 %gather.51 = (bf16[2,8,4,2,128,128]{5,4,3,2,1,0:T(8,128)(2,1)}, bf16[2,2,8,128,128]{4,3,2,1,0:T(8,128)(2,1)S(1)}) custom-call(bf16[2,8,128,512]{3,2,1,0:T(8,128)(2,1)} %data.20), custom_call_target="tpu_custom_call" | custom-call | tf_op jit(solution)/shard_map/cond/branch_20_fun/gather/pallas_call | solution.py:263
  66.1 0.0 copy-done
  66.1 6.0 %multiply.1 = bf16[16,128,512]{2,1,0:T(8,128)(2,1)} custom-call(f32[2,8]{1,0:T(2,128)S(1)} %copy-done, bf16[2,8,4,2,128,128]{5,4,3,2,1,0:T(8,128)(2,1)} %get-tuple-element.38.rows_hbm, bf16[2,2,8,128,128]{4,3,2,1,0:T(8,128)(2,1)S(1)} %get-tuple-element.39.cols), custom_call_target="tpu_custom_call" | custom-call | tf_op jit(solution)/shard_map/multiply/pallas_call | solution.py:374
Async XLA Ops:
  1.9 64.2 %copy-start = (f32[2,8]{1,0:T(2,128)S(1)}, f32[2,8]{1,0:T(2,128)}, u32[]{:S(2)}) copy-start(f32[2,8]{1,0:T(2,128)} %wave.1) | copy-start | bytes 196
